TPU v7x, 32 devices: a whole 2x2x4 slice. The times are simulated.
32 devices in a mesh: seq: 16 (over z, y, core), tp: 2 (over x).
Axes of the slice: x: 2, y: 2, z: 4, core: 2. Of those that a mesh axis runs over, the one named last changes fastest.
Arguments:
- queries: bfloat16 [4096, 4096], P('seq', 'tp'), may hold values from -6 to 6, as said below
- keys: bfloat16 [4096, 512], P('seq', 'tp'), may hold values from -6 to 6, as said below
- values: bfloat16 [4096, 512], P('seq', 'tp'), may hold values from -6 to 6
- segment: int32 [4096], P('seq'), may hold values from 0 to 31, never falling along the last dimension, each value on 1 to 512 neighbouring positions
- repack: int32 [4096], P('seq'), may hold values from 0 to 4095, as said below
- proj: bfloat16 [1536, 4096], P('seq', 'tp'), may hold values from -0.5 to 0.5
- student_states: bfloat16 [4096, 1536], P('seq'), may hold values from -6 to 6
- target_row: int32 [4096], P('seq'), may hold values from 0 to 255
Outputs:
- student_rows: bfloat16 [4096, 1536], P('seq', 'tp')
- grad: float32 [1536, 4096], P('seq', 'tp')
Inputs may be any that keep to these rules, and one draw needn't show every extreme that they name: `queries`: scaled normal entries. `keys`: scaled normal entries. `repack`: A permutation of the student rows. Each device's teacher rows go in consecutive groups of 32 rows, in order, each group to one student owner (the device holding student rows owner * 256 to owner * 256 + 255); every device sends exactly 32 rows to each of 8 other devices and none to itself, so at most 32 rows from one device to one owner, reached by every sending pair.
All inputs are finite; a program needn't handle non-finite values.
Results may differ from a plain program's by a relative error of at most 0.0056.
Values may be sent and summed in bfloat16 or wider, within the bound.
A program may use at most 64 MiB of HBM per device.

v0:
```python
import math

import jax
import jax.numpy as jnp
from jax import lax
from jax.sharding import PartitionSpec as P

HEADS = 32
KV_HEADS = 4
HEAD_DIM = 128
SW = 1536
REACH = 2


neg_large = -1e30


def prefix(value, axis, combine, identity):
    size, here = (lax.axis_size(axis), lax.axis_index(axis))
    everything = jax.tree.map(lambda part: lax.all_gather(part, axis), value)
    start = jax.tree.map(
        lambda part, zero: jnp.broadcast_to(jnp.asarray(zero, part.dtype), part.shape),
        value,
        identity,
    )

    def hop(k, before):
        reached = k < here
        new = combine(before, jax.tree.map(lambda part: part[k], everything))
        return jax.tree.map(lambda a, b: jnp.where(reached, a, b), new, before)

    return lax.fori_loop(0, size, hop, start)


def passed_along(block, axis, distance):
    devices = range(lax.axis_size(axis))
    route = [(i - distance, i) for i in devices if i - distance in devices]
    return lax.ppermute(block, axis, route)


def anchor_combine(earlier, later):
    first_id = jnp.where(earlier[0] < 0, later[0], earlier[0])
    last_id = jnp.where(later[1] < 0, earlier[1], later[1])
    whole_later = (later[0] == later[1]) & (later[0] == earlier[1]) & (later[0] >= 0)
    start_pos = jnp.where(later[1] < 0, earlier[2], jnp.where(whole_later, earlier[2], later[2]))
    return (first_id, last_id, start_pos)


def document_starts(segment):
    row_count = segment.shape[0]
    row_pos = lax.axis_index("seq") * row_count + jnp.arange(row_count, dtype=jnp.int32)
    first_id = segment[0]
    last_id = segment[-1]
    last_start = jnp.min(jnp.where(segment == last_id, row_pos, jnp.int32(2**30)))
    sentinel = jnp.int32(-1)
    carried = prefix(
        (first_id, last_id, last_start), "seq", anchor_combine, (sentinel, sentinel, sentinel)
    )
    is_new = jnp.concatenate([jnp.ones((1,), bool), segment[1:] != segment[:-1]])
    local_start = lax.cummax(jnp.where(is_new, row_pos, jnp.int32(-1)), axis=0)
    inherit = (segment == carried[1]) & (segment == first_id)
    return (jnp.where(inherit, carried[2], local_start), row_pos)


def attend(queries, keys, values, row_start, row_pos):
    row_count = queries.shape[0]
    key_list = [keys]
    value_list = [values]
    pos_list = [row_pos]
    for step in range(1, REACH + 1):
        earlier = passed_along((keys, values), "seq", step)
        key_list.insert(0, earlier[0])
        value_list.insert(0, earlier[1])
        pos_list.insert(0, row_pos - step * row_count)
    all_keys = jnp.concatenate(key_list, axis=0)
    all_values = jnp.concatenate(value_list, axis=0)
    key_pos = jnp.concatenate(pos_list, axis=0)
    allowed = (key_pos[None, :] >= row_start[:, None]) & (key_pos[None, :] <= row_pos[:, None])
    kv_local = keys.shape[1] // HEAD_DIM
    group = HEADS // KV_HEADS
    part_size = 1
    q_heads = queries.reshape(row_count, kv_local, group, HEAD_DIM)
    scale = 1.0 / math.sqrt(HEAD_DIM)
    outputs = []
    for head in range(kv_local):
        key_head = all_keys[:, head * HEAD_DIM : (head + 1) * HEAD_DIM]
        value_head = all_values[:, head * HEAD_DIM : (head + 1) * HEAD_DIM]
        for first in range(0, group, part_size):
            q_part = q_heads[:, head, first : first + part_size, :]
            scores = (
                jnp.einsum("tjd,sd->jts", q_part, key_head, preferred_element_type=jnp.float32)
                * scale
            )
            scores = jnp.where(allowed[None], scores, neg_large)
            top = jnp.max(scores, axis=-1, keepdims=True)
            expo = jnp.exp(scores - top)
            weights = (expo / jnp.sum(expo, axis=-1, keepdims=True)).astype(jnp.bfloat16)
            mixed = jnp.einsum(
                "jts,sd->tjd", weights, value_head, preferred_element_type=jnp.float32
            )
            outputs.append(mixed.astype(jnp.bfloat16))
    return jnp.concatenate(outputs, axis=1).reshape(row_count, -1)


def project_rows(row_data, proj):
    return jnp.einsum(
        "tf,nf->tn",
        row_data,
        lax.all_gather(proj, "seq", axis=0, tiled=True),
        preferred_element_type=jnp.float32,
    )


def fill_buckets(data, target_dev, slot_rank, devices, capacity):
    empty = jnp.zeros((devices, capacity, data.shape[1]), data.dtype)
    return empty.at[target_dev, slot_rank].set(data)


def place_rows(received, slots, row_count):
    width = received.shape[-1]
    holder = jnp.zeros((row_count + 1, width), received.dtype)
    holder = holder.at[slots.reshape(-1)].set(received.reshape(-1, width))
    return holder[:row_count]


def on_device(queries, keys, values, segment, repack, proj, student_states, target_row):
    row_count = queries.shape[0]
    devices = lax.axis_size("seq")
    row_start, row_pos = document_starts(segment)
    attended = attend(queries, keys, values, row_start, row_pos)
    capacity = max(2 * row_count // devices, 2)
    target_dev = repack // row_count
    local_slot = repack - target_dev * row_count
    same_dev = target_dev[:, None] == target_dev[None, :]
    row_ids = jnp.arange(row_count, dtype=jnp.int32)
    before = row_ids[None, :] < row_ids[:, None]
    slot_rank = jnp.sum((same_dev & before).astype(jnp.int32), axis=1)
    slot_table = (
        jnp.full((devices, capacity), row_count, jnp.int32)
        .at[target_dev, slot_rank]
        .set(local_slot)
    )
    width_share = SW // lax.axis_size("tp")
    tp_index = lax.axis_index("tp")
    targets = student_states[target_row]
    target_share = lax.dynamic_slice_in_dim(targets, tp_index * width_share, width_share, 1)
    y_part = project_rows(attended, proj)
    y_share = lax.psum_scatter(y_part, "tp", scatter_dimension=1, tiled=True).astype(jnp.bfloat16)
    buckets = fill_buckets(y_share, target_dev, slot_rank, devices, capacity)
    arrived = (
        lax.all_to_all(buckets, "seq", split_axis=0, concat_axis=0, tiled=True),
        lax.all_to_all(slot_table, "seq", split_axis=0, concat_axis=0, tiled=True),
    )
    out_rows = place_rows(arrived[0], arrived[1], row_count)
    delta_share = (out_rows.astype(jnp.float32) - target_share.astype(jnp.float32)).astype(
        jnp.bfloat16
    )
    padded = jnp.concatenate([delta_share, jnp.zeros((1, width_share), jnp.bfloat16)], axis=0)
    returned = lax.all_to_all(padded[arrived[1]], "seq", split_axis=0, concat_axis=0, tiled=True)
    delta_teacher = returned[target_dev, slot_rank]
    delta = lax.all_gather(delta_teacher, "tp", axis=1, tiled=True)
    norm_factor = 1.0 / math.sqrt(row_count * devices)
    grad_rows = delta.shape[1] // devices
    term = jnp.einsum("ts,tf->sf", delta, attended, preferred_element_type=jnp.float32)
    pieces = term.reshape(devices, grad_rows, term.shape[1])
    summed = lax.all_to_all(
        pieces.astype(jnp.bfloat16), "seq", split_axis=0, concat_axis=0, tiled=True
    ).astype(pieces.dtype)
    grad = jnp.sum(summed, axis=0) * norm_factor
    return (out_rows, grad)


def solution(mesh):
    placed = (
        P("seq", "tp"),
        P("seq", "tp"),
        P("seq", "tp"),
        P("seq"),
        P("seq"),
        P("seq", "tp"),
        P("seq", None),
        P("seq"),
    )
    return jax.shard_map(
        on_device,
        mesh=mesh,
        in_specs=placed,
        out_specs=(P("seq", "tp"), P("seq", "tp")),
        check_vma=False,
    )
```

profile of v0, /device:TPU:0, one launch (start us, length us, event | category | flops | bytes accessed | tf_op | source)
XLA Modules:
  0.0 485.2 jit_solution(7615775658288469235)
XLA Ops:
  7.2 5.0 %collective-permute-start.2 = (bf16[256,256]{1,0:T(8,128)(2,1)}, bf16[256,256]{1,0:T(8,128)(2,1)S(1)}, u32[]{:S(2)}, u32[]{:S(2)}) collective-permute-start(bf16[256,256]{1,0:T(8,128)(2,1)} %param.11), channel_id=1, source_target_pairs={{0,4},{2,6},{4,8},{6,10},{8,12},{10,14},{12,16},{14,18},{16,20},{1... | collective-permute-start | bytes 393224 | tf_op jit(solution)/shard_map/ppermute | solution.py:38
  12.2 1.5 collective-permute-start.3
  13.7 3.9 collective-permute-start
  17.6 3.3 collective-permute-start.1
  21.0 0.8 slice_compare_fusion
  21.8 1.2 dynamic-slice
  23.0 2.0 fusion.153
  25.0 1.4 slice_dynamic-update-slice_fusion
  26.5 2.0 fusion.149
  28.6 1.4 dynamic-update-slice.2
  29.9 9.5 %all-reduce.4 = (s32[16]{0:T(128)S(1)}, s32[16]{0:T(128)S(1)}, s32[16]{0:T(128)S(1)}) all-reduce(s32[16]{0:T(128)S(1)} %get-tuple-element.153, s32[16]{0:T(128)S(1)} %slice_dynamic-update-slice_fusion, s32[16]{0:T(128)S(1)} %dynamic-update-slice.2), channel_id=1, replica_groups=mesh['seq'=16,'tp'=2] {'seq'}, use_global_device_ids=true, to_apply=%add.1 | all-reduce | flops 48 | bytes 384
  39.9 97.8 %while.15 = (s32[]{:T(128)}, s32[]{:T(128)}, s32[]{:T(128)}, s32[]{:T(128)}, s32[16]{0:T(128)S(1)}, /*index=5*/s32[16]{0:T(128)S(1)}, s32[16]{0:T(128)S(1)}, s32[]{:T(128)}, s32[]{:T(128)}) while((s32[]{:T(128)}, s32[]{:T(128)}, s32[]{:T(128)}, s32[]{:T(128)}, s32[16]{0:T(128)S(1)}, /*index=5*/s32[16]{0:T(128)S(1)}, s32[16]{0:T(128)S(1)}, ...), condition=%wide.region_4.5_spmd, body=%wide.region_3.4_spmd.sunk | while | flops 14 | bytes 261 | solution.py:32
  44.7 0.6 dynamic_slice.31
  50.8 0.6 dynamic_slice.31
  56.9 0.6 dynamic_slice.31
  63.0 0.6 dynamic_slice.31
  69.2 0.6 dynamic_slice.31
  75.3 0.6 dynamic_slice.31
  81.4 0.6 dynamic_slice.31
  87.5 0.6 dynamic_slice.31
  93.6 0.6 dynamic_slice.31
  99.7 0.6 dynamic_slice.31
  105.8 0.6 dynamic_slice.31
  124.2 0.6 dynamic_slice.31
  137.8 1.3 and_select_fusion
  139.1 2.3 copy.54
  141.5 0.9 constant_dynamic-update-slice_fusion.3
  142.5 1.0 constant_dynamic-update-slice_fusion
  143.5 1.2 fusion.154
  144.9 1.3 fusion.155
  146.3 1.3 fusion.156
  147.8 1.3 fusion.157
  149.2 1.2 fusion.158
  150.6 1.3 fusion.159
  152.0 1.3 fusion.160
  153.5 1.3 fusion.161
  154.9 1.3 fusion.162
  156.3 1.3 fusion.163
  157.8 1.3 fusion.164
  159.2 1.3 fusion.165
  160.6 1.3 fusion.166
  162.1 1.3 fusion.167
  163.5 1.3 fusion.168
  164.9 1.2 fusion.169
  171.0 5.8 %fusion.170 = f32[256,1536]{1,0:T(8,128)} fusion(bf16[256,2048]{0,1:T(8,128)(2,1)S(1)} %bitcast.400, bf16[1536,2048]{1,0:T(8,128)(2,1)} %all-gather.2.cloned.1.call-done), kind=kOutput, calls=%fused_computation.292 | convolution fusion | flops 1610612736 | bytes 8912896 | tf_op jit(solution)/shard_map/tf,nf->tn/dot_general | solution.py:106
  177.6 39.3 %scatter_fusion = s32[16,32]{1,0:T(8,128)} fusion(s32[16,32]{1,0:T(8,128)} %broadcast_in_dim.41, s32[256]{0:T(256)S(1)} %bitcast.378, s32[256]{0:T(256)S(1)} %get-tuple-element.148), kind=kCustom, calls=%fused_computation.3 | custom fusion | bytes 5120 | tf_op jit(solution)/shard_map/scatter | solution.py:141
  217.0 5.1 %all-to-all-start = ((s32[16,1,32]{2,1,0:T(1,128)}), s32[16,1,32]{2,1,0:T(1,128)S(1)}, u32[]{:S(2)}, u32[]{:S(2)}) async-start(s32[16,1,32]{2,1,0:T(1,128)} %bitcast.7), calls=%async_computation | async-start | bytes 16384 | tf_op jit(solution)/shard_map/all_to_all | solution.py:152
  222.2 1.2 convert_element_type.278
  223.3 1.0 broadcast_in_dim.43
  224.3 38.0 %scatter_fusion.1 = bf16[16,32,768]{2,1,0:T(8,128)(2,1)} fusion(bf16[16,32,768]{2,1,0:T(8,128)(2,1)} %broadcast_in_dim.43, s32[256]{0:T(256)S(1)} %bitcast.379, bf16[256,768]{1,0:T(8,128)(2,1)S(1)} %convert_element_type.278), kind=kCustom, calls=%fused_computation.4 | custom fusion | bytes 1181696 | tf_op jit(solution)/shard_map/scatter | solution.py:116
  262.3 5.9 %all-to-all-start.1 = ((bf16[16,32,768]{2,1,0:T(8,128)(2,1)}), bf16[16,32,768]{2,1,0:T(8,128)(2,1)}, u32[]{:S(2)}, u32[]{:S(2)}) async-start(bf16[16,32,768]{2,1,0:T(8,128)(2,1)} %scatter_fusion.1), calls=%async_computation.2 | async-start | bytes 1572864 | tf_op jit(solution)/shard_map/all_to_all | solution.py:151
  268.2 1.3 gather_fusion
  270.0 0.7 reduce.37
  270.9 16.1 %all-to-all-done.1 = bf16[16,32,768]{2,1,0:T(8,128)(2,1)} async-done(((bf16[16,32,768]{2,1,0:T(8,128)(2,1)}), bf16[16,32,768]{2,1,0:T(8,128)(2,1)}, u32[]{:S(2)}, u32[]{:S(2)}) %all-to-all-start.1) | async-done | bytes 786464 | tf_op jit(solution)/shard_map/all_to_all | solution.py:151
  287.0 3.3 scatter_custom_fusion.2
  290.2 0.9 subtract_convert_fusion
  291.1 2.0 gather_fusion.1
  293.2 25.5 %all_to_all.27 = bf16[16,32,768]{2,1,0:T(8,128)(2,1)S(1)} all-to-all(bf16[16,32,768]{2,1,0:T(8,128)(2,1)S(1)} %bitcast.382), channel_id=1, replica_groups=mesh['seq'=16,'tp'=2] {'seq'}, dimensions={0} | all-to-all | bytes 1572864 | tf_op jit(solution)/shard_map/all_to_all | solution.py:159
  318.7 2.4 gather_fusion.2
  321.1 12.5 %all_gather.23 = bf16[256,1536]{1,0:T(8,128)(2,1)S(1)} all-gather(bf16[256,768]{1,0:T(8,128)(2,1)S(1)} %gather_fusion.2), channel_id=1, replica_groups=mesh['seq'=16,'tp'=2] {'tp'}, dimensions={1}, use_global_device_ids=true | all-gather | bytes 1179648 | tf_op jit(solution)/shard_map/all_gather | solution.py:161
  333.9 1.8 convolution_convert_fusion
  335.7 140.4 %all_to_all.28 = bf16[16,96,2048]{2,1,0:T(8,128)(2,1)S(1)} all-to-all(bf16[16,96,2048]{2,1,0:T(8,128)(2,1)S(1)} %convolution_convert_fusion), channel_id=1, replica_groups=mesh['seq'=16,'tp'=2] {'seq'}, dimensions={0} | all-to-all | bytes 12582912 | tf_op jit(solution)/shard_map/all_to_all | solution.py:166
  476.2 1.3 convert_reduce_fusion
  477.4 1.0 broadcast_multiply_fusion
  (117 shorter events, 31.5 us)
Async XLA Ops:
  7.2 261.1 %copy-start = (bf16[256,1536]{1,0:T(8,128)(2,1)S(1)}, bf16[256,1536]{1,0:T(8,128)(2,1)}, u32[]{:S(2)}) copy-start(bf16[256,1536]{1,0:T(8,128)(2,1)} %param.16) | copy-start | bytes 2359300
  7.2 163.8 %all-gather.2.cloned.1.call-start = ((), (), s32[]{:S(2)}) async-start(), calls=%async_computation.5 | async-start | bytes 6684672 | tf_op jit(solution)/shard_map/all_gather | solution.py:109
  7.2 134.2 %collective-permute-start.2 = (bf16[256,256]{1,0:T(8,128)(2,1)}, bf16[256,256]{1,0:T(8,128)(2,1)S(1)}, u32[]{:S(2)}, u32[]{:S(2)}) collective-permute-start(bf16[256,256]{1,0:T(8,128)(2,1)} %param.11), channel_id=1, source_target_pairs={{0,4},{2,6},{4,8},{6,10},{8,12},{10,14},{12,16},{14,18},{16,20},{1... | collective-permute-start | bytes 393224 | tf_op jit(solution)/shard_map/ppermute | solution.py:38
  12.2 129.2 %collective-permute-start.3 = (bf16[256,256]{1,0:T(8,128)(2,1)}, bf16[256,256]{1,0:T(8,128)(2,1)S(1)}, u32[]{:S(2)}, u32[]{:S(2)}) collective-permute-start(bf16[256,256]{1,0:T(8,128)(2,1)} %param.11), channel_id=1, source_target_pairs={{0,2},{2,4},{4,6},{6,8},{8,10},{10,12},{12,14},{14,16},{16,18},{18... | collective-permute-start | bytes 393224 | tf_op jit(solution)/shard_map/ppermute | solution.py:38
  13.7 128.7 %collective-permute-start = (bf16[256,256]{1,0:T(8,128)(2,1)}, bf16[256,256]{1,0:T(8,128)(2,1)S(1)}, u32[]{:S(2)}, u32[]{:S(2)}) collective-permute-start(bf16[256,256]{1,0:T(8,128)(2,1)} %param.12), channel_id=1, source_target_pairs={{0,4},{2,6},{4,8},{6,10},{8,12},{10,14},{12,16},{14,18},{16,20},{1... | collective-permute-start | bytes 393224 | tf_op jit(solution)/shard_map/ppermute | solution.py:38
  17.6 124.8 %collective-permute-start.1 = (bf16[256,256]{1,0:T(8,128)(2,1)}, bf16[256,256]{1,0:T(8,128)(2,1)S(1)}, u32[]{:S(2)}, u32[]{:S(2)}) collective-permute-start(bf16[256,256]{1,0:T(8,128)(2,1)} %param.12), channel_id=1, source_target_pairs={{0,2},{2,4},{4,6},{6,8},{8,10},{10,12},{12,14},{14,16},{16,18},{18... | collective-permute-start | bytes 393224 | tf_op jit(solution)/shard_map/ppermute | solution.py:38
  20.9 201.3 %reduce-scatter.2.cloned.1.call-start = ((), (), s32[]{:S(2)}) async-start(), calls=%async_computation.6 | async-start | bytes 2359296 | tf_op jit(solution)/shard_map/reduce_scatter | solution.py:148
  142.4 1.1 copy-start.1
  171.0 5.9 %copy-start.2 = (s32[256]{0:T(256)S(1)}, s32[256]{0:T(256)}, u32[]{:S(2)}) copy-start(s32[256]{0:T(256)} %param.14) | copy-start | bytes 3076
  177.6 90.6 %copy-start.3 = (s32[256]{0:T(256)S(1)}, s32[256]{0:T(256)}, u32[]{:S(2)}) copy-start(s32[256]{0:T(256)} %param.17) | copy-start | bytes 3076
  217.0 45.3 %all-to-all-start = ((s32[16,1,32]{2,1,0:T(1,128)}), s32[16,1,32]{2,1,0:T(1,128)S(1)}, u32[]{:S(2)}, u32[]{:S(2)}) async-start(s32[16,1,32]{2,1,0:T(1,128)} %bitcast.7), calls=%async_computation | async-start | bytes 16384 | tf_op jit(solution)/shard_map/all_to_all | solution.py:152
  262.3 24.7 %all-to-all-start.1 = ((bf16[16,32,768]{2,1,0:T(8,128)(2,1)}), bf16[16,32,768]{2,1,0:T(8,128)(2,1)}, u32[]{:S(2)}, u32[]{:S(2)}) async-start(bf16[16,32,768]{2,1,0:T(8,128)(2,1)} %scatter_fusion.1), calls=%async_computation.2 | async-start | bytes 1572864 | tf_op jit(solution)/shard_map/all_to_all | solution.py:151
Sparse Core Ops, SparseCore 0:
  21.0 61.3 all-gather.1
  176.9 26.4 reduce-scatter.1
where the time goes:
time: 490 us; the launch traced here: 485 us
  blocking collectives  188 us (38%)
  local copies, waits for them, and re-layouts  128 us (26%)
  loops' own time  68.8 us (14%)
  matrix products  32.1 us (7%)
  starting transfers between devices  24.7 us (5%)
  waiting for transfers between devices  16.2 us (3%)
  between operations  14.6 us (3%)
  other arithmetic  12.5 us (3%)
    all_to_all x1, blocking collectives, on_device(): lax.all_to_all(pieces.astype(jnp.bfloat16), 'seq', split_axis=0, concat_a...  140 us
    another operation x1, loops' own time, prefix(): return lax.fori_loop(0, size, hop, start)  68.8 us
    scatter x1, local copies, waits for them, and re-layouts, on_device(): slot_table = jnp.full((devices, capacity), row_count, jnp.int32).at[targe...  39.3 us
    scatter x1, local copies, waits for them, and re-layouts, fill_buckets(): return empty.at[target_dev, slot_rank].set(data)  38 us
    dynamic_slice x48, local copies, waits for them, and re-layouts, hop(): new = combine(before, jax.tree.map(lambda part: part[k], everything))  29 us
    all_to_all x1, blocking collectives, on_device(): lax.all_to_all(padded[arrived[1]], 'seq', split_axis=0, concat_axis=0, ti...  25.5 us
    dot_general x16, matrix products, attend(): jnp.einsum('tjd,sd->jts', q_part, key_head, preferred_element_type=jnp.fl...  20 us
    all_to_all x1, waiting for transfers between devices, on_device(): lax.all_to_all(buckets, 'seq', split_axis=0, concat_axis=0, tiled=True)  16.1 us
  transfers between devices with their start and end apart: 8, of which 1 were waited for; matrix products, arithmetic and copies ran while one was open for 32% of the time, Pallas kernels for 0%

commit v1 on v0

v1 whole, which is shorter than its diff:
```python
import functools
import math

import jax
import jax.numpy as jnp
from jax import lax
from jax.experimental import pallas as pl
from jax.experimental.pallas import tpu as pltpu
from jax.sharding import PartitionSpec as P

HEADS = 32
KV_HEADS = 4
HEAD_DIM = 128
SW = 1536
REACH = 2

neg_large = -1e30


def attention_kernel(q_ref, *refs):
    blocks = REACH + 1
    k_refs, v_refs = refs[:blocks], refs[blocks : 2 * blocks]
    seg_q_ref, seg_k_ref, out_ref, bias = refs[2 * blocks :]
    rows = q_ref.shape[0]
    before = REACH * rows

    @pl.when(pl.program_id(0) == 0)
    def _():
        q_pos = lax.broadcasted_iota(jnp.int32, bias.shape, 0) + before
        k_pos = lax.broadcasted_iota(jnp.int32, bias.shape, 1)
        allowed = (seg_q_ref[...] == seg_k_ref[...]) & (k_pos <= q_pos)
        bias[...] = jnp.where(allowed, 0.0, neg_large)

    scale = math.log2(math.e) / math.sqrt(HEAD_DIM)
    keys = jnp.concatenate([ref[...] for ref in k_refs], axis=0)
    values = jnp.concatenate([ref[...] for ref in v_refs], axis=0)
    scores = lax.dot_general(
        q_ref[...], keys, (((1,), (1,)), ((), ())), preferred_element_type=jnp.float32
    )
    scores = scores * scale + bias[...]
    top = jnp.max(scores, axis=-1, keepdims=True)
    expo = jnp.exp2(scores - top)
    total = jnp.sum(expo, axis=-1, keepdims=True)
    mixed = jnp.dot(expo.astype(jnp.bfloat16), values, preferred_element_type=jnp.float32)
    out_ref[...] = (mixed / total).astype(out_ref.dtype)


def attend(queries, key_list, value_list, seg_q, seg_k):
    rows, width = queries.shape
    group = HEADS // KV_HEADS
    head_spec = pl.BlockSpec((rows, HEAD_DIM), lambda h: (0, h))
    kv_spec = pl.BlockSpec((rows, HEAD_DIM), lambda h: (0, h // group))
    span = seg_k.shape[1]
    heads = width // HEAD_DIM
    return pl.pallas_call(
        attention_kernel,
        grid=(heads,),
        out_shape=jax.ShapeDtypeStruct(queries.shape, jnp.bfloat16),
        in_specs=[head_spec]
        + [kv_spec] * (2 * (REACH + 1))
        + [
            pl.BlockSpec((rows, 1), lambda h: (0, 0)),
            pl.BlockSpec((1, span), lambda h: (0, 0)),
        ],
        out_specs=head_spec,
        scratch_shapes=[pltpu.VMEM((rows, span), jnp.float32)],
        compiler_params=pltpu.CompilerParams(
            dimension_semantics=("arbitrary",), vmem_limit_bytes=24 * 1024 * 1024
        ),
        cost_estimate=pl.CostEstimate(
            flops=4 * heads * rows * span * HEAD_DIM,
            bytes_accessed=6 * rows * width,
            transcendentals=heads * rows * span,
        ),
    )(queries, *key_list, *value_list, seg_q, seg_k)


def bf16_dot(a, b, contract):
    return lax.dot_general(a, b, (contract, ((), ())), preferred_element_type=jnp.float32)


def select(mask, rows):
    return jnp.dot(
        mask.astype(jnp.bfloat16), rows, preferred_element_type=jnp.float32
    ).astype(jnp.bfloat16)


def on_device(queries, keys, values, segment, repack, proj, student_states, target_row):
    bf16 = jnp.bfloat16
    row_count = queries.shape[0]
    devices, tp_size = lax.axis_size("seq"), lax.axis_size("tp")
    here, tp_index = lax.axis_index("seq"), lax.axis_index("tp")
    core = lax.rem(here, 2)
    chips = devices // 2
    same_core = [[2 * k + c for k in range(chips)] for c in range(2)]
    swap = [(i, i ^ 1) for i in range(devices)]
    capacity = max(2 * row_count // devices, 2)
    groups = row_count // capacity
    share = SW // tp_size
    half = share // 2
    piece = proj.shape[0]
    features = proj.shape[1]

    def to_partner(block):
        return lax.ppermute(block, "seq", swap)

    table = lax.all_gather(jnp.stack([segment, repack]), "seq", axis=0)
    whole_proj = lax.all_gather(proj, "seq", axis=0, tiled=True, axis_index_groups=same_core)

    key_list, value_list = [keys], [values]
    for step in range(1, REACH + 1):
        route = [(i - step, i) for i in range(step, devices)]
        earlier_k, earlier_v = lax.ppermute((keys, values), "seq", route)
        key_list.insert(0, earlier_k)
        value_list.insert(0, earlier_v)
    seg_list = []
    for step in range(REACH, 0, -1):
        earlier = lax.dynamic_index_in_dim(table, jnp.maximum(here - step, 0), 0, False)[0]
        seg_list.append(jnp.where(here >= step, earlier, -1))
    seg_k = jnp.concatenate(seg_list + [segment])[None, :]

    repack_all = table[:, 1]
    owner_all = repack_all // row_count
    mine = (owner_all == here).reshape(devices, groups, capacity)
    local = (repack_all - here * row_count).reshape(devices, groups, capacity)
    slots = jnp.max(jnp.where(mine, local, -1), axis=1).reshape(-1)
    row_ids = jnp.arange(row_count, dtype=jnp.int32)
    bucket = (repack // row_count) * capacity + row_ids % capacity
    bucket_ids = jnp.arange(devices * capacity, dtype=jnp.int32)

    blocks = half // piece
    states = lax.dynamic_slice_in_dim(student_states, tp_index * share, share, 1)
    states = states.reshape(row_count, blocks, 2, piece).transpose(0, 2, 1, 3)
    states = states.reshape(row_count, share)
    targets = select(target_row[:, None] == row_ids[None, :], states)
    outgoing = select(slots[:, None] == row_ids[None, :], targets)
    incoming = lax.all_to_all(
        outgoing.reshape(devices, capacity, share), "seq", split_axis=0, concat_axis=0, tiled=True
    ).reshape(devices * capacity, share)
    own_target = select(bucket[:, None] == bucket_ids[None, :], incoming)
    even, odd = own_target[:, :half], own_target[:, half:]
    target_keep = jnp.where(core == 0, even, odd)
    target_give = jnp.where(core == 0, odd, even)
    target = jnp.concatenate([target_keep, to_partner(target_give)], axis=0)

    attended = attend(queries, key_list, value_list, segment[:, None], seg_k)
    both = jnp.concatenate([attended, to_partner(attended)], axis=0)

    y_part = bf16_dot(both, whole_proj, ((1,), (1,)))
    y_sum = lax.dynamic_slice_in_dim(y_part, tp_index * half, half, 1)
    for shift in range(1, tp_size):
        route = [(i, (i + shift) % tp_size) for i in range(tp_size)]
        to = lax.rem(tp_index + shift, tp_size)
        give = lax.dynamic_slice_in_dim(y_part, to * half, half, 1).astype(bf16)
        y_sum = y_sum + lax.ppermute(give, "tp", route).astype(jnp.float32)
    y_share = y_sum.astype(bf16)
    delta_share = (y_share.astype(jnp.float32) - target.astype(jnp.float32)).astype(bf16)
    delta = lax.all_gather(delta_share, "tp", axis=1, tiled=True)

    y_own, y_other = y_share[:row_count], to_partner(y_share[row_count:])
    y_even = jnp.where(core == 0, y_own, y_other).reshape(row_count, blocks, 1, piece)
    y_odd = jnp.where(core == 0, y_other, y_own).reshape(row_count, blocks, 1, piece)
    y_rows = jnp.concatenate([y_even, y_odd], axis=2).reshape(row_count, share)
    buckets = select(bucket_ids[:, None] == bucket[None, :], y_rows)
    arrived = lax.all_to_all(
        buckets.reshape(devices, capacity, share), "seq", split_axis=0, concat_axis=0, tiled=True
    ).reshape(devices * capacity, share)
    out_rows = select(row_ids[:, None] == slots[None, :], arrived)

    term = bf16_dot(delta, both, ((0,), (0,)))
    summed = lax.psum_scatter(
        term.astype(bf16).reshape(chips * piece, features),
        "seq",
        scatter_dimension=0,
        tiled=True,
        axis_index_groups=same_core,
    )
    grad = summed.astype(jnp.float32) * (1.0 / math.sqrt(row_count * devices))
    return (out_rows, grad)


def solution(mesh):
    placed = (
        P("seq", "tp"),
        P("seq", "tp"),
        P("seq", "tp"),
        P("seq"),
        P("seq"),
        P("seq", "tp"),
        P("seq", None),
        P("seq"),
    )
    return jax.shard_map(
        on_device,
        mesh=mesh,
        in_specs=placed,
        out_specs=(P("seq", "tp"), P("seq", "tp")),
        check_vma=False,
    )
```

time: 490 us -> 240 us (0.49)
  local copies, waits for them, and re-layouts: 128 us -> 4.11 us
  blocking collectives: 188 us -> 97.4 us
  loops' own time: 68.8 us -> 0 us
  waiting for transfers between devices: 16.2 us -> 68.2 us
  matrix products: 32.1 us -> 13.5 us
  Pallas kernels: 0 us -> 11.4 us
  other arithmetic: 12.5 us -> 4.85 us
    all_to_all x2 -> x1, blocking collectives: 166 us -> 63.2 us  [on_device(): lax.all_to_all(buckets.reshape(devices, capacity, share), 'seq', split_ax...]
    scatter x3 -> x0, local copies, waits for them, and re-layouts: 80.6 us -> none  [the longest x1 39.3 us: on_device(): slot_table = jnp.full((devices, capacity), row_count, jnp.int32).at[targe...]
    another operation x1 -> x0, loops' own time: 68.8 us -> none  [prefix(): return lax.fori_loop(0, size, hop, start)]
    reduce_scatter x1, waiting for transfers between devices: 0.02 us -> 47.1 us  [on_device(): lax.psum_scatter(term.astype(bf16).reshape(chips * piece, features), 'seq...]
    dynamic_slice x48 -> x1, local copies, waits for them, and re-layouts: 29 us -> 0.03 us  [on_device(): lax.dynamic_slice_in_dim(student_states, tp_index * share, share, 1)]
    all_gather x1 -> x2, blocking collectives: 12.5 us -> 34.1 us  [the longest x1 23.3 us: on_device(): table = lax.all_gather(jnp.stack([segment, repack]), 'seq', axis=0)]
    ppermute x4 -> x8, waiting for transfers between devices: 0.01 us -> 18.8 us  [the longest x4 7.68 us: on_device(): earlier_k, earlier_v = lax.ppermute((keys, values), 'seq', route)]
    dot_general x34 -> x6, matrix products: 32.1 us -> 13.5 us  [the longest x2 8.83 us: bf16_dot(): lax.dot_general(a, b, (contract, ((), ())), preferred_element_type=jnp.fl...]
  transfers between devices with their start and end apart: 8 -> 11, of which waited for: 1 -> 7; matrix products, arithmetic and copies ran while one was open for 32% -> 3% of each run, Pallas kernels for 0% -> 5%
where the time goes in v1:
time: 240 us
  blocking collectives  97.4 us (41%)
  waiting for transfers between devices  68.2 us (28%)
  starting transfers between devices  26 us (11%)
  between operations  14.4 us (6%)
  matrix products  13.5 us (6%)
  Pallas kernels  11.4 us (5%)
  other arithmetic  4.85 us (2%)
  local copies, waits for them, and re-layouts  4.11 us (2%)
    all_to_all x1, blocking collectives, on_device(): lax.all_to_all(buckets.reshape(devices, capacity, share), 'seq', split_ax...  63.2 us
    reduce_scatter x1, waiting for transfers between devices, on_device(): lax.psum_scatter(term.astype(bf16).reshape(chips * piece, features), 'seq...  47.1 us
    all_gather x1, blocking collectives, on_device(): table = lax.all_gather(jnp.stack([segment, repack]), 'seq', axis=0)  23.3 us
    ppermute x4, starting transfers between devices, on_device(): earlier_k, earlier_v = lax.ppermute((keys, values), 'seq', route)  12.2 us
    pallas_call x1, Pallas kernels, attend(): pl.pallas_call(attention_kernel, grid=(heads,), out_shape=jax.ShapeDtypeS...  11.4 us
    all_gather x1, blocking collectives, on_device(): delta = lax.all_gather(delta_share, 'tp', axis=1, tiled=True)  10.9 us
    dot_general x2, matrix products, bf16_dot(): lax.dot_general(a, b, (contract, ((), ())), preferred_element_type=jnp.fl...  8.83 us
    ppermute x3, starting transfers between devices, to_partner(): return lax.ppermute(block, 'seq', swap)  7.86 us
  transfers between devices with their start and end apart: 11, of which 7 were waited for; matrix products, arithmetic and copies ran while one was open for 3% of the time, Pallas kernels for 5%

profile of v1, /device:TPU:0, one launch (start us, length us, event | category | flops | bytes accessed | tf_op | source)
XLA Modules:
  0.0 239.8 jit_solution(2529784044422862593)
XLA Ops:
  7.2 0.0 copy-start
  7.2 0.0 copy-start.11
  7.2 0.0 all-gather.4.cloned.1.call-start
  7.2 0.7 all-gather.4.cloned.1.call-update
  7.9 0.7 add_bitcast_fusion
  8.6 23.3 %all-gather.1 = s32[16,2,256]{2,1,0:T(2,128)S(1)} all-gather(s32[1,2,256]{2,1,0:T(2,128)S(1)} %add_bitcast_fusion), channel_id=2, replica_groups=mesh['seq'=16,'tp'=2] {'seq'}, dimensions={0}, use_global_device_ids=true | all-gather | bytes 34816 | tf_op jit(solution)/shard_map/all_gather | solution.py:107
  32.0 0.1 squeeze.8
  32.0 0.1 select_reduce_fusion
  32.1 0.1 eq.89
  32.2 0.0 copy-done
  32.2 0.0 copy-start.2
  32.2 0.0 copy-start.3
  32.3 0.0 copy-start.9
  32.3 0.0 copy-start.1
  32.3 0.2 copy.22
  32.5 0.0 copy-done.11
  32.5 1.5 convolution_convert_fusion.1
  34.0 4.3 %all-to-all-start.1 = ((bf16[16,32,768]{2,1,0:T(8,128)(2,1)}), bf16[16,32,768]{2,1,0:T(8,128)(2,1)}, u32[]{:S(2)}, u32[]{:S(2)}) async-start(bf16[16,32,768]{2,1,0:T(8,128)(2,1)} %bitcast.14), calls=%async_computation.1 | async-start | bytes 1572864 | tf_op jit(solution)/shard_map/all_to_all | solution.py:137
  38.3 0.0 reduce-scatter.2.cloned.1.call-start
  38.4 0.0 copy-done.2
  38.4 3.7 %collective-permute-start = (bf16[256,256]{1,0:T(8,128)(2,1)S(1)}, bf16[256,256]{1,0:T(8,128)(2,1)S(1)}, u32[]{:S(2)}, u32[]{:S(2)}) collective-permute-start(bf16[256,256]{1,0:T(8,128)(2,1)S(1)} %copy-done.2), channel_id=1, source_target_pairs={{0,4},{2,6},{4,8},{6,10},{8,12},{10,14},{12,16},{14,18},{16,20},{1... | collective-permute-start | bytes 393224 | tf_op jit(solution)/shard_map/ppermute | solution.py:113
  42.1 1.8 collective-permute-start.1
  43.8 0.0 copy-done.3
  43.9 3.5 %collective-permute-start.2 = (bf16[256,256]{1,0:T(8,128)(2,1)S(1)}, bf16[256,256]{1,0:T(8,128)(2,1)S(1)}, u32[]{:S(2)}, u32[]{:S(2)}) collective-permute-start(bf16[256,256]{1,0:T(8,128)(2,1)S(1)} %copy-done.3), channel_id=1, source_target_pairs={{0,4},{2,6},{4,8},{6,10},{8,12},{10,14},{12,16},{14,18},{16,20},{1... | collective-permute-start | bytes 393224 | tf_op jit(solution)/shard_map/ppermute | solution.py:113
  47.4 3.2 %collective-permute-start.3 = (bf16[256,256]{1,0:T(8,128)(2,1)S(1)}, bf16[256,256]{1,0:T(8,128)(2,1)S(1)}, u32[]{:S(2)}, u32[]{:S(2)}) collective-permute-start(bf16[256,256]{1,0:T(8,128)(2,1)S(1)} %copy-done.3), channel_id=1, source_target_pairs={{0,2},{2,4},{4,6},{6,8},{8,10},{10,12},{12,14},{14,16},{16,18},{18... | collective-permute-start | bytes 393224 | tf_op jit(solution)/shard_map/ppermute | solution.py:113
  50.6 0.0 copy-done.9
  50.7 0.0 copy-start.10
  50.7 0.1 copy.16.refs_6_
  50.8 0.0 collective-permute-done.refs_0_
  50.8 0.0 collective-permute-done.1.refs_1_
  50.9 7.7 %collective-permute-done.2.refs_3_ = bf16[256,256]{1,0:T(8,128)(2,1)S(1)} collective-permute-done((bf16[256,256]{1,0:T(8,128)(2,1)S(1)}, bf16[256,256]{1,0:T(8,128)(2,1)S(1)}, u32[]{:S(2)}, u32[]{:S(2)}) %collective-permute-start.2) | collective-permute-done | bytes 131104 | tf_op jit(solution)/shard_map/ppermute | solution.py:113
  58.5 0.7 copy-done.4
  59.2 0.0 collective-permute-done.3.refs_4_
  59.2 0.6 copy-done.6
  59.8 0.0 copy-done.1
  59.8 0.9 copy-done.5
  60.7 0.9 copy-done.7
  61.6 11.4 %shard_map.95 = bf16[256,2048]{1,0:T(8,128)(2,1)S(1)} custom-call(bf16[256,2048]{1,0:T(8,128)(2,1)S(1)} %copy-done.1, bf16[256,256]{1,0:T(8,128)(2,1)S(1)} %collective-permute-done.refs_0_, bf16[256,256]{1,0:T(8,128)(2,1)S(1)} %collective-permute-done.1.refs_1_, bf16[256,256]{1,0:T(8,128)(2,1)S(1)} %copy-done.2, bf16[256,256]{1,0:T(8,128)(2,1)S(1)} %copy-done.5, ...), custom_call_target="tpu_custom_call" | custom-call | flops 1610612736 | bytes 3145728 | tf_op jit(solution)/shard_map/pallas_call | solution.py:55
  73.1 7.8 %collective-permute-start.4 = (bf16[256,2048]{1,0:T(8,128)(2,1)S(1)}, bf16[256,2048]{1,0:T(8,128)(2,1)}, u32[]{:S(2)}, u32[]{:S(2)}) collective-permute-start(bf16[256,2048]{1,0:T(8,128)(2,1)S(1)} %shard_map.95), channel_id=1, source_target_pairs={{0,2},{2,0},{4,6},{6,4},{8,10},{10,8},{12,14},{14,12},{16,18},{18,... | collective-permute-start | bytes 3145736 | tf_op jit(solution)/shard_map/ppermute | solution.py:105
  80.9 0.0 copy-done.10
  80.9 0.0 all-to-all-done.1
  80.9 1.5 convolution_convert_fusion.3
  82.4 0.8 collective-permute-done.4
  83.3 1.6 all-gather.4.cloned.1.call-done
  84.9 4.1 %fusion = f32[512,768]{1,0:T(8,128)S(1)} fusion(bf16[768,2048]{1,0:T(8,128)(2,1)} %all-gather.4.cloned.1.call-done, bf16[256,2048]{1,0:T(8,128)(2,1)} %collective-permute-done.4, bf16[256,2048]{1,0:T(8,128)(2,1)S(1)} %shard_map.95), kind=kOutput, calls=%fused_computation.4 | convolution fusion | flops 1614807040 | bytes 6815744 | tf_op jit(solution)/shard_map/dot_general | solution.py:79
  89.1 0.1 dynamic-slice_convert_fusion
  89.1 1.6 collective-permute-start.5
  90.7 0.7 broadcast_select_fusion.1
  91.4 0.0 collective-permute-start.7
  91.4 1.6 collective-permute-done.7
  93.0 7.2 %collective-permute-done.5 = bf16[512,384]{1,0:T(8,128)(2,1)S(1)} collective-permute-done((bf16[512,384]{1,0:T(8,128)(2,1)S(1)}, bf16[512,384]{1,0:T(8,128)(2,1)S(1)}, u32[]{:S(2)}, u32[]{:S(2)}) %collective-permute-start.5) | collective-permute-done | bytes 393248 | tf_op jit(solution)/shard_map/ppermute | solution.py:155
  100.2 1.3 subtract_convert_fusion
  101.5 10.9 %all_gather.15 = bf16[512,768]{1,0:T(8,128)(2,1)S(1)} all-gather(bf16[512,384]{1,0:T(8,128)(2,1)S(1)} %get-tuple-element.2), channel_id=1, replica_groups=mesh['seq'=16,'tp'=2] {'tp'}, dimensions={1}, use_global_device_ids=true | all-gather | bytes 1179648 | tf_op jit(solution)/shard_map/all_gather | solution.py:158
  112.4 4.7 %convolution_convert_fusion = bf16[768,2048]{1,0:T(8,128)(2,1)} fusion(bf16[512,768]{1,0:T(8,128)(2,1)S(1)} %all_gather.15, bf16[256,2048]{1,0:T(8,128)(2,1)} %collective-permute-done.4, bf16[256,2048]{1,0:T(8,128)(2,1)S(1)} %shard_map.95), kind=kOutput, calls=%fused_computation | convolution fusion | flops 1616379904 | bytes 6029312 | tf_op jit(solution)/shard_map/dot_general | solution.py:79
  117.1 0.0 reduce-scatter.2.cloned.1.call-update
  117.2 0.1 collective-permute-start.6
  117.2 1.4 collective-permute-done.6
  118.7 0.1 copy.17
  118.9 0.1 copy.18
  119.1 0.4 convolution_convert_fusion.2
  119.5 63.2 %all_to_all.10 = bf16[16,32,768]{2,1,0:T(8,128)(2,1)S(1)} all-to-all(bf16[16,32,768]{2,1,0:T(8,128)(2,1)S(1)} %bitcast.25), channel_id=1, replica_groups=mesh['seq'=16,'tp'=2] {'seq'}, dimensions={0} | all-to-all | bytes 1572864 | tf_op jit(solution)/shard_map/all_to_all | solution.py:165
  182.7 1.1 convolution_convert_fusion.5
  183.9 47.1 %reduce-scatter.2.cloned.1.call-done = bf16[96,2048]{1,0:T(8,128)(2,1)} async-done(((bf16[768,2048]{1,0:T(8,128)(2,1)}), bf16[96,2048]{1,0:T(8,128)(2,1)}) %reduce-scatter.2.cloned.1.call-update) | async-done | bytes 393232 | tf_op jit(solution)/shard_map/reduce_scatter | solution.py:171
  231.0 1.9 convert_multiply_fusion
  (17 shorter events, 0.3 us)
Async XLA Ops:
  7.2 25.0 %copy-start = (bf16[256,1536]{1,0:T(8,128)(2,1)S(1)}, bf16[256,1536]{1,0:T(8,128)(2,1)}, u32[]{:S(2)}) copy-start(bf16[256,1536]{1,0:T(8,128)(2,1)} %param.14) | copy-start | bytes 2359300
  7.2 25.3 %copy-start.11 = (s32[256]{0:T(256)S(1)}, s32[256]{0:T(256)}, u32[]{:S(2)}) copy-start(s32[256]{0:T(256)} %param.15) | copy-start | bytes 3076
  7.2 77.7 %all-gather.4.cloned.1.call-start = ((), (), s32[]{:S(2)}) async-start(), calls=%async_computation.3 | async-start | bytes 3538944 | tf_op jit(solution)/shard_map/all_gather | solution.py:108
  32.2 6.1 %copy-start.2 = (bf16[256,256]{1,0:T(8,128)(2,1)S(1)}, bf16[256,256]{1,0:T(8,128)(2,1)}, u32[]{:S(2)}) copy-start(bf16[256,256]{1,0:T(8,128)(2,1)} %refs_2_.1) | copy-start | bytes 393220
  32.2 11.6 %copy-start.3 = (bf16[256,256]{1,0:T(8,128)(2,1)S(1)}, bf16[256,256]{1,0:T(8,128)(2,1)}, u32[]{:S(2)}) copy-start(bf16[256,256]{1,0:T(8,128)(2,1)} %refs_5_.1) | copy-start | bytes 393220
  32.3 18.4 %copy-start.9 = (s32[256]{0:T(256)S(1)}, s32[256]{0:T(256)}, u32[]{:S(2)}) copy-start(s32[256]{0:T(256)} %param.11) | copy-start | bytes 3076
  32.3 27.6 %copy-start.1 = (bf16[256,2048]{1,0:T(8,128)(2,1)S(1)}, bf16[256,2048]{1,0:T(8,128)(2,1)}, u32[]{:S(2)}) copy-start(bf16[256,2048]{1,0:T(8,128)(2,1)} %q_ref.1) | copy-start | bytes 3145732
  34.0 46.8 %all-to-all-start.1 = ((bf16[16,32,768]{2,1,0:T(8,128)(2,1)}), bf16[16,32,768]{2,1,0:T(8,128)(2,1)}, u32[]{:S(2)}, u32[]{:S(2)}) async-start(bf16[16,32,768]{2,1,0:T(8,128)(2,1)} %bitcast.14), calls=%async_computation.1 | async-start | bytes 1572864 | tf_op jit(solution)/shard_map/all_to_all | solution.py:137
  38.3 192.7 %reduce-scatter.2.cloned.1.call-start = ((), (), s32[]{:S(2)}) async-start(), calls=%async_computation.4 | async-start | bytes 3538944 | tf_op jit(solution)/shard_map/reduce_scatter | solution.py:171
  38.4 12.4 %collective-permute-start = (bf16[256,256]{1,0:T(8,128)(2,1)S(1)}, bf16[256,256]{1,0:T(8,128)(2,1)S(1)}, u32[]{:S(2)}, u32[]{:S(2)}) collective-permute-start(bf16[256,256]{1,0:T(8,128)(2,1)S(1)} %copy-done.2), channel_id=1, source_target_pairs={{0,4},{2,6},{4,8},{6,10},{8,12},{10,14},{12,16},{14,18},{16,20},{1... | collective-permute-start | bytes 393224 | tf_op jit(solution)/shard_map/ppermute | solution.py:113
  42.1 8.8 %collective-permute-start.1 = (bf16[256,256]{1,0:T(8,128)(2,1)S(1)}, bf16[256,256]{1,0:T(8,128)(2,1)S(1)}, u32[]{:S(2)}, u32[]{:S(2)}) collective-permute-start(bf16[256,256]{1,0:T(8,128)(2,1)S(1)} %copy-done.2), channel_id=1, source_target_pairs={{0,2},{2,4},{4,6},{6,8},{8,10},{10,12},{12,14},{14,16},{16,18},{18... | collective-permute-start | bytes 393224 | tf_op jit(solution)/shard_map/ppermute | solution.py:113
  43.9 14.7 %collective-permute-start.2 = (bf16[256,256]{1,0:T(8,128)(2,1)S(1)}, bf16[256,256]{1,0:T(8,128)(2,1)S(1)}, u32[]{:S(2)}, u32[]{:S(2)}) collective-permute-start(bf16[256,256]{1,0:T(8,128)(2,1)S(1)} %copy-done.3), channel_id=1, source_target_pairs={{0,4},{2,6},{4,8},{6,10},{8,12},{10,14},{12,16},{14,18},{16,20},{1... | collective-permute-start | bytes 393224 | tf_op jit(solution)/shard_map/ppermute | solution.py:113
  47.4 11.8 %collective-permute-start.3 = (bf16[256,256]{1,0:T(8,128)(2,1)S(1)}, bf16[256,256]{1,0:T(8,128)(2,1)S(1)}, u32[]{:S(2)}, u32[]{:S(2)}) collective-permute-start(bf16[256,256]{1,0:T(8,128)(2,1)S(1)} %copy-done.3), channel_id=1, source_target_pairs={{0,2},{2,4},{4,6},{6,8},{8,10},{10,12},{12,14},{14,16},{16,18},{18... | collective-permute-start | bytes 393224 | tf_op jit(solution)/shard_map/ppermute | solution.py:113
  50.7 30.2 %copy-start.10 = (s32[256]{0:T(256)S(1)}, s32[256]{0:T(256)}, u32[]{:S(2)}) copy-start(s32[256]{0:T(256)} %param.12) | copy-start | bytes 3076
  58.5 0.7 copy-start.4
  59.2 0.6 copy-start.6
  59.8 0.9 copy-start.5
  60.7 0.9 copy-start.7
  73.1 10.2 %collective-permute-start.4 = (bf16[256,2048]{1,0:T(8,128)(2,1)S(1)}, bf16[256,2048]{1,0:T(8,128)(2,1)}, u32[]{:S(2)}, u32[]{:S(2)}) collective-permute-start(bf16[256,2048]{1,0:T(8,128)(2,1)S(1)} %shard_map.95), channel_id=1, source_target_pairs={{0,2},{2,0},{4,6},{6,4},{8,10},{10,8},{12,14},{14,12},{16,18},{18,... | collective-permute-start | bytes 3145736 | tf_op jit(solution)/shard_map/ppermute | solution.py:105
  89.0 2.3 copy-start.8
  89.1 11.1 %collective-permute-start.5 = (bf16[512,384]{1,0:T(8,128)(2,1)S(1)}, bf16[512,384]{1,0:T(8,128)(2,1)S(1)}, u32[]{:S(2)}, u32[]{:S(2)}) collective-permute-start(bf16[512,384]{1,0:T(8,128)(2,1)S(1)} %dynamic-slice_convert_fusion), channel_id=1, source_target_pairs={{0,1},{1,0},{2,3},{3,2},{4,5},{5,4},{6,7},{7,6},{8,9},{9,8},{10,11... | collective-permute-start | bytes 1179656 | tf_op jit(solution)/shard_map/ppermute | solution.py:155
  91.4 1.7 collective-permute-start.7
  117.2 1.5 collective-permute-start.6
Sparse Core Ops, SparseCore 0:
  10.2 74.6 all-gather.3
  117.2 113.6 reduce-scatter.1

commit v2 on v1

--- a/solution.py
+++ b/solution.py
@@ -85,6 +85,130 @@
     ).astype(jnp.bfloat16)
 
 
+def scatter_kernel(seq_size, delta_ref, rows_ref, out_ref, *scratch):
+    send_y, recv_y, send_r, recv_r, send_l, recv_l, sem_y, sem_r, sem_l = scratch
+    here, tp_index = lax.axis_index("seq"), lax.axis_index("tp")
+    line = seq_size // 4
+    core = here % 2
+    y = (here // 2) % 2
+    z = here // 4
+    piece = out_ref.shape[0]
+
+    def device(z_to, y_to):
+        return ((z_to * 2 + y_to) * 2 + core, tp_index)
+
+    def copy(src, dst, sems, slot, to):
+        return pltpu.make_async_remote_copy(
+            src_ref=src.at[slot],
+            dst_ref=dst.at[slot],
+            send_sem=sems.at[0, slot],
+            recv_sem=sems.at[1, slot],
+            device_id=to,
+            device_id_type=pl.DeviceIdType.MESH,
+        )
+
+    def to_y(slot):
+        return copy(send_y, recv_y, sem_y, slot, device(z, 1 - y))
+
+    def to_right(slot):
+        return copy(send_r, recv_r, sem_r, slot, device((z + 1) % line, y))
+
+    def to_left(slot):
+        return copy(send_l, recv_l, sem_l, slot, device((z + line - 1) % line, y))
+
+    def term(z_of, y_of):
+        first = pl.multiple_of((z_of * 2 + y_of) * piece, piece)
+        return jnp.dot(
+            delta_ref[pl.ds(first, piece), :], rows_ref[...], preferred_element_type=jnp.float32
+        )
+
+    has_left, has_right = z > 0, z < line - 1
+    barrier = pltpu.get_barrier_semaphore()
+
+    def greet(to):
+        pl.semaphore_signal(barrier, inc=1, device_id=to, device_id_type=pl.DeviceIdType.MESH)
+
+    greet(device(z, 1 - y))
+    pl.when(has_left)(lambda: greet(device(z - 1, y)))
+    pl.when(has_right)(lambda: greet(device(z + 1, y)))
+    peers = 1 + has_left.astype(jnp.int32) + has_right.astype(jnp.int32)
+    pl.semaphore_wait(barrier, peers)
+
+    def start_y(slot):
+        send_y[slot] = term(slot, 1 - y).astype(jnp.bfloat16)
+        to_y(slot).start()
+
+    def summed(slot):
+        own = term(slot, y)
+        to_y(slot).wait_recv()
+        return own + recv_y[slot].astype(jnp.float32)
+
+    def pass_right(slot):
+        send_r[slot] = summed(slot).astype(jnp.bfloat16)
+
+        @pl.when(has_left)
+        def _():
+            to_right(slot).wait_recv()
+            added = send_r[slot].astype(jnp.float32) + recv_r[slot].astype(jnp.float32)
+            send_r[slot] = added.astype(jnp.bfloat16)
+
+        to_right(slot).start()
+
+    def pass_left(slot):
+        send_l[slot] = summed(slot).astype(jnp.bfloat16)
+
+        @pl.when(has_right)
+        def _():
+            to_left(slot).wait_recv()
+            added = send_l[slot].astype(jnp.float32) + recv_l[slot].astype(jnp.float32)
+            send_l[slot] = added.astype(jnp.bfloat16)
+
+        to_left(slot).start()
+
+    def farthest_first(right, left):
+        for distance in range(line - 1, 0, -1):
+            pl.when(z + distance < line)(lambda: right(z + distance))
+            pl.when(z - distance >= 0)(lambda: left(z - distance))
+
+    farthest_first(start_y, start_y)
+    start_y(z)
+    farthest_first(pass_right, pass_left)
+    out_ref[...] = summed(z)
+
+    @pl.when(has_left)
+    def _():
+        to_right(z).wait_recv()
+        out_ref[...] += recv_r[z].astype(jnp.float32)
+
+    @pl.when(has_right)
+    def _():
+        to_left(z).wait_recv()
+        out_ref[...] += recv_l[z].astype(jnp.float32)
+
+    for slot in range(line):
+        to_y(slot).wait_send()
+    farthest_first(lambda slot: to_right(slot).wait_send(), lambda slot: to_left(slot).wait_send())
+
+
+def scatter_terms(delta_rows, rows, seq_size):
+    line = seq_size // 4
+    piece, width = delta_rows.shape[0] // (seq_size // 2), rows.shape[1]
+    return pl.pallas_call(
+        functools.partial(scatter_kernel, seq_size),
+        out_shape=jax.ShapeDtypeStruct((piece, width), jnp.float32),
+        in_specs=[pl.BlockSpec(memory_space=pltpu.VMEM)] * 2,
+        out_specs=pl.BlockSpec(memory_space=pltpu.VMEM),
+        scratch_shapes=[pltpu.VMEM((line, piece, width), jnp.bfloat16)] * 6
+        + [pltpu.SemaphoreType.DMA((2, line))] * 3,
+        compiler_params=pltpu.CompilerParams(
+            collective_id=0, has_side_effects=True, vmem_limit_bytes=40 * 1024 * 1024
+        ),
+        cost_estimate=pl.CostEstimate(
+            flops=2 * delta_rows.size * width, bytes_accessed=rows.size * 2, transcendentals=0
+        ),
+    )(delta_rows, rows)
+
+
 def on_device(queries, keys, values, segment, repack, proj, student_states, target_row):
     bf16 = jnp.bfloat16
     row_count = queries.shape[0]
@@ -167,15 +291,18 @@
     ).reshape(devices * capacity, share)
     out_rows = select(row_ids[:, None] == slots[None, :], arrived)
 
-    term = bf16_dot(delta, both, ((0,), (0,)))
-    summed = lax.psum_scatter(
-        term.astype(bf16).reshape(chips * piece, features),
-        "seq",
-        scatter_dimension=0,
-        tiled=True,
-        axis_index_groups=same_core,
-    )
-    grad = summed.astype(jnp.float32) * (1.0 / math.sqrt(row_count * devices))
+    if devices % 4 == 0 and devices <= 32 and piece % 16 == 0:
+        summed = scatter_terms(delta.T, both, devices)
+    else:
+        term = bf16_dot(delta, both, ((0,), (0,)))
+        summed = lax.psum_scatter(
+            term.astype(bf16).reshape(chips * piece, features),
+            "seq",
+            scatter_dimension=0,
+            tiled=True,
+            axis_index_groups=same_core,
+        ).astype(jnp.float32)
+    grad = summed * (1.0 / math.sqrt(row_count * devices))
     return (out_rows, grad)
 
 

time: 240 us -> 199 us (0.83)
  blocking collectives: 97.4 us -> 35.4 us
  waiting for transfers between devices: 68.2 us -> 21.9 us
  Pallas kernels: 11.4 us -> 54.1 us
  starting transfers between devices: 26 us -> 53.7 us
  matrix products: 13.5 us -> 9.34 us
    all_to_all x1 -> x0, blocking collectives: 63.2 us -> none  [on_device(): lax.all_to_all(buckets.reshape(devices, capacity, share), 'seq', split_ax...]
    reduce_scatter x1 -> x0, waiting for transfers between devices: 47.1 us -> none  [on_device(): lax.psum_scatter(term.astype(bf16).reshape(chips * piece, features), 'seq...]
    pallas_call x0 -> x1, Pallas kernels: none -> 42.6 us  [scatter_terms(): pl.pallas_call(functools.partial(scatter_kernel, seq_size), out_shape=jax...]
    all_to_all x0 -> x1, starting transfers between devices: none -> 27.8 us  [on_device(): lax.all_to_all(buckets.reshape(devices, capacity, share), 'seq', split_ax...]
    dot_general x2 -> x1, matrix products: 8.83 us -> 3.72 us  [bf16_dot(): lax.dot_general(a, b, (contract, ((), ())), preferred_element_type=jnp.fl...]
  transfers between devices with their start and end apart: 11 -> 11, of which waited for: 7 -> 6; matrix products, arithmetic and copies ran while one was open for 3% -> 4% of each run, Pallas kernels for 5% -> 27%
where the time goes in v2:
time: 199 us; the launch traced here: 198 us
  Pallas kernels  54.1 us (27%)
  starting transfers between devices  53.7 us (27%)
  blocking collectives  35.4 us (18%)
  waiting for transfers between devices  21.9 us (11%)
  between operations  14.4 us (7%)
  matrix products  9.34 us (5%)
  other arithmetic  4.75 us (2%)
  local copies, waits for them, and re-layouts  4.63 us (2%)
    pallas_call x1, Pallas kernels, scatter_terms(): pl.pallas_call(functools.partial(scatter_kernel, seq_size), out_shape=jax...  42.6 us
    all_to_all x1, starting transfers between devices, on_device(): lax.all_to_all(buckets.reshape(devices, capacity, share), 'seq', split_ax...  27.8 us
    all_gather x1, blocking collectives, on_device(): table = lax.all_gather(jnp.stack([segment, repack]), 'seq', axis=0)  23.3 us
    ppermute x4, starting transfers between devices, on_device(): earlier_k, earlier_v = lax.ppermute((keys, values), 'seq', route)  12.2 us
    all_gather x1, blocking collectives, on_device(): delta = lax.all_gather(delta_share, 'tp', axis=1, tiled=True)  12.1 us
    pallas_call x1, Pallas kernels, attend(): pl.pallas_call(attention_kernel, grid=(heads,), out_shape=jax.ShapeDtypeS...  11.4 us
    ppermute x1, waiting for transfers between devices, on_device(): y_sum = y_sum + lax.ppermute(give, 'tp', route).astype(jnp.float32)  8.21 us
    ppermute x3, starting transfers between devices, to_partner(): return lax.ppermute(block, 'seq', swap)  7.88 us
  transfers between devices with their start and end apart: 11, of which 6 were waited for; matrix products, arithmetic and copies ran while one was open for 4% of the time, Pallas kernels for 27%

profile of v2, /device:TPU:0, one launch (start us, length us, event | category | flops | bytes accessed | tf_op | source)
XLA Modules:
  0.0 198.1 jit_solution(8899812554202435959)
XLA Ops:
  7.2 0.0 copy-start
  7.2 0.0 copy-start.12
  7.2 0.0 all-gather.4.cloned.1.call-start
  7.2 0.7 all-gather.4.cloned.1.call-update
  7.9 0.7 add_bitcast_fusion
  8.6 23.3 %all-gather.1 = s32[16,2,256]{2,1,0:T(2,128)S(1)} all-gather(s32[1,2,256]{2,1,0:T(2,128)S(1)} %add_bitcast_fusion), channel_id=2, replica_groups=mesh['seq'=16,'tp'=2] {'seq'}, dimensions={0}, use_global_device_ids=true | all-gather | bytes 34816 | tf_op jit(solution)/shard_map/all_gather | solution.py:231
  32.0 0.1 squeeze.8
  32.0 0.1 select_reduce_fusion
  32.1 0.1 eq.89
  32.2 0.0 copy-done
  32.2 0.0 copy-start.2
  32.2 0.0 copy-start.3
  32.3 0.0 copy-start.10
  32.3 0.0 copy-start.1
  32.3 0.2 copy.31
  32.5 0.0 copy-done.12
  32.5 1.5 convolution_convert_fusion
  34.0 4.3 %all-to-all-start.1 = ((bf16[16,32,768]{2,1,0:T(8,128)(2,1)}), bf16[16,32,768]{2,1,0:T(8,128)(2,1)}, u32[]{:S(2)}, u32[]{:S(2)}) async-start(bf16[16,32,768]{2,1,0:T(8,128)(2,1)} %bitcast.16), calls=%async_computation.1 | async-start | bytes 1572864 | tf_op jit(solution)/shard_map/all_to_all | solution.py:261
  38.3 0.0 copy-done.2
  38.3 3.7 %collective-permute-start = (bf16[256,256]{1,0:T(8,128)(2,1)S(1)}, bf16[256,256]{1,0:T(8,128)(2,1)S(1)}, u32[]{:S(2)}, u32[]{:S(2)}) collective-permute-start(bf16[256,256]{1,0:T(8,128)(2,1)S(1)} %copy-done.2), channel_id=1, source_target_pairs={{0,4},{2,6},{4,8},{6,10},{8,12},{10,14},{12,16},{14,18},{16,20},{1... | collective-permute-start | bytes 393224 | tf_op jit(solution)/shard_map/ppermute | solution.py:237
  42.0 1.8 collective-permute-start.1
  43.8 0.0 copy-done.3
  43.8 3.5 %collective-permute-start.2 = (bf16[256,256]{1,0:T(8,128)(2,1)S(1)}, bf16[256,256]{1,0:T(8,128)(2,1)S(1)}, u32[]{:S(2)}, u32[]{:S(2)}) collective-permute-start(bf16[256,256]{1,0:T(8,128)(2,1)S(1)} %copy-done.3), channel_id=1, source_target_pairs={{0,4},{2,6},{4,8},{6,10},{8,12},{10,14},{12,16},{14,18},{16,20},{1... | collective-permute-start | bytes 393224 | tf_op jit(solution)/shard_map/ppermute | solution.py:237
  47.3 3.2 %collective-permute-start.3 = (bf16[256,256]{1,0:T(8,128)(2,1)S(1)}, bf16[256,256]{1,0:T(8,128)(2,1)S(1)}, u32[]{:S(2)}, u32[]{:S(2)}) collective-permute-start(bf16[256,256]{1,0:T(8,128)(2,1)S(1)} %copy-done.3), channel_id=1, source_target_pairs={{0,2},{2,4},{4,6},{6,8},{8,10},{10,12},{12,14},{14,16},{16,18},{18... | collective-permute-start | bytes 393224 | tf_op jit(solution)/shard_map/ppermute | solution.py:237
  50.6 0.0 copy-done.10
  50.6 0.0 copy-start.11
  50.6 0.1 copy.21.refs_6_
  50.8 0.0 collective-permute-done.refs_0_
  50.8 0.0 collective-permute-done.1.refs_1_
  50.8 7.7 %collective-permute-done.2.refs_3_ = bf16[256,256]{1,0:T(8,128)(2,1)S(1)} collective-permute-done((bf16[256,256]{1,0:T(8,128)(2,1)S(1)}, bf16[256,256]{1,0:T(8,128)(2,1)S(1)}, u32[]{:S(2)}, u32[]{:S(2)}) %collective-permute-start.2) | collective-permute-done | bytes 131104 | tf_op jit(solution)/shard_map/ppermute | solution.py:237
  58.5 0.0 copy-start.4
  58.5 0.7 copy-done.4
  59.2 0.0 collective-permute-done.3.refs_4_
  59.2 0.6 copy-done.6
  59.8 0.0 copy-done.1
  59.8 0.9 copy-done.5
  60.7 0.9 copy-done.7
  61.6 11.4 %shard_map.95 = bf16[256,2048]{1,0:T(8,128)(2,1)S(1)} custom-call(bf16[256,2048]{1,0:T(8,128)(2,1)S(1)} %copy-done.1, bf16[256,256]{1,0:T(8,128)(2,1)S(1)} %collective-permute-done.refs_0_, bf16[256,256]{1,0:T(8,128)(2,1)S(1)} %collective-permute-done.1.refs_1_, bf16[256,256]{1,0:T(8,128)(2,1)S(1)} %copy-done.2, bf16[256,256]{1,0:T(8,128)(2,1)S(1)} %copy-done.5, ...), custom_call_target="tpu_custom_call" | custom-call | flops 1610612736 | bytes 3145728 | tf_op jit(solution)/shard_map/pallas_call | solution.py:55
  73.1 7.7 %collective-permute-start.4 = (bf16[256,2048]{1,0:T(8,128)(2,1)S(1)}, bf16[256,2048]{1,0:T(8,128)(2,1)S(1)}, u32[]{:S(2)}, u32[]{:S(2)}) collective-permute-start(bf16[256,2048]{1,0:T(8,128)(2,1)S(1)} %shard_map.95), channel_id=1, source_target_pairs={{0,2},{2,0},{4,6},{6,4},{8,10},{10,8},{12,14},{14,12},{16,18},{18,... | collective-permute-start | bytes 3145736 | tf_op jit(solution)/shard_map/ppermute | solution.py:229
  80.8 0.0 copy-done.11
  80.8 0.0 all-to-all-done.1
  80.8 1.7 convolution_convert_fusion.2
  82.5 0.6 collective-permute-done.4
  83.1 1.8 all-gather.4.cloned.1.call-done
  84.9 3.7 %fusion.10 = f32[512,768]{0,1:T(8,128)S(1)} fusion(bf16[768,2048]{1,0:T(8,128)(2,1)} %all-gather.4.cloned.1.call-done, bf16[256,2048]{1,0:T(8,128)(2,1)S(1)} %collective-permute-done.4, bf16[256,2048]{1,0:T(8,128)(2,1)S(1)} %shard_map.95), kind=kOutput, calls=%fused_computation.48 | convolution fusion | flops 1614807040 | bytes 6815744 | tf_op jit(solution)/shard_map/dot_general | solution.py:79
  88.6 0.0 copy-done.8
  88.6 0.0 copy-start.9
  88.6 0.9 dynamic-slice_convert_fusion
  89.5 1.5 collective-permute-start.5
  91.1 0.0 copy-done.9
  91.1 0.1 collective-permute-start.7
  91.2 1.4 collective-permute-done.7
  92.6 8.2 %collective-permute-done.5 = bf16[512,384]{0,1:T(8,128)(2,1)S(1)} collective-permute-done((bf16[512,384]{0,1:T(8,128)(2,1)}, bf16[512,384]{0,1:T(8,128)(2,1)S(1)}, u32[]{:S(2)}, u32[]{:S(2)}) %collective-permute-start.5) | collective-permute-done | bytes 393248 | tf_op jit(solution)/shard_map/ppermute | solution.py:279
  100.8 1.3 subtract_convert_fusion
  102.1 0.1 collective-permute-start.6
  102.2 1.4 collective-permute-done.6
  103.7 1.3 convolution_convert_fusion.1
  105.0 27.8 %all-to-all-start = ((bf16[16,32,768]{2,1,0:T(8,128)(2,1)}), bf16[16,32,768]{2,1,0:T(8,128)(2,1)S(1)}, u32[]{:S(2)}, u32[]{:S(2)}) async-start(bf16[16,32,768]{2,1,0:T(8,128)(2,1)} %bitcast.11), calls=%async_computation | async-start | bytes 1572864 | tf_op jit(solution)/shard_map/all_to_all | solution.py:289
  132.9 1.6 pad_maximum_fusion.rows_ref
  134.4 12.1 %all_gather.15 = bf16[512,768]{0,1:T(8,128)(2,1)S(1)} all-gather(bf16[512,384]{0,1:T(8,128)(2,1)S(1)} %get-tuple-element.2), channel_id=1, replica_groups=mesh['seq'=16,'tp'=2] {'tp'}, dimensions={1}, use_global_device_ids=true | all-gather | bytes 1179648 | tf_op jit(solution)/shard_map/all_gather | solution.py:282
  146.6 42.6 %shard_map.96 = f32[96,2048]{1,0:T(8,128)S(1)} custom-call(bf16[768,512]{1,0:T(8,128)(2,1)S(1)} %bitcast.28, bf16[512,2048]{1,0:T(8,128)(2,1)S(1)} %pad_maximum_fusion.rows_ref), custom_call_target="tpu_custom_call" | custom-call | flops 1610612736 | bytes 2097152 | tf_op jit(solution)/shard_map/pallas_call | solution.py:196
  189.2 1.0 broadcast_multiply_fusion
  190.2 0.0 all-to-all-done
  190.2 1.1 convolution_convert_fusion.4
  (15 shorter events, 0.3 us)
Async XLA Ops:
  7.2 25.0 %copy-start = (bf16[256,1536]{1,0:T(8,128)(2,1)S(1)}, bf16[256,1536]{1,0:T(8,128)(2,1)}, u32[]{:S(2)}) copy-start(bf16[256,1536]{1,0:T(8,128)(2,1)} %param.14) | copy-start | bytes 2359300
  7.2 25.3 %copy-start.12 = (s32[256]{0:T(256)S(1)}, s32[256]{0:T(256)}, u32[]{:S(2)}) copy-start(s32[256]{0:T(256)} %param.15) | copy-start | bytes 3076
  7.2 77.7 %all-gather.4.cloned.1.call-start = ((), (), s32[]{:S(2)}) async-start(), calls=%async_computation.2 | async-start | bytes 3538944 | tf_op jit(solution)/shard_map/all_gather | solution.py:232
  32.2 6.1 %copy-start.2 = (bf16[256,256]{1,0:T(8,128)(2,1)S(1)}, bf16[256,256]{1,0:T(8,128)(2,1)}, u32[]{:S(2)}) copy-start(bf16[256,256]{1,0:T(8,128)(2,1)} %refs_2_.1) | copy-start | bytes 393220
  32.2 11.6 %copy-start.3 = (bf16[256,256]{1,0:T(8,128)(2,1)S(1)}, bf16[256,256]{1,0:T(8,128)(2,1)}, u32[]{:S(2)}) copy-start(bf16[256,256]{1,0:T(8,128)(2,1)} %refs_5_.1) | copy-start | bytes 393220
  32.3 18.3 %copy-start.10 = (s32[256]{0:T(256)S(1)}, s32[256]{0:T(256)}, u32[]{:S(2)}) copy-start(s32[256]{0:T(256)} %param.11) | copy-start | bytes 3076
  32.3 27.6 %copy-start.1 = (bf16[256,2048]{1,0:T(8,128)(2,1)S(1)}, bf16[256,2048]{1,0:T(8,128)(2,1)}, u32[]{:S(2)}) copy-start(bf16[256,2048]{1,0:T(8,128)(2,1)} %q_ref.1) | copy-start | bytes 3145732
  34.0 46.8 %all-to-all-start.1 = ((bf16[16,32,768]{2,1,0:T(8,128)(2,1)}), bf16[16,32,768]{2,1,0:T(8,128)(2,1)}, u32[]{:S(2)}, u32[]{:S(2)}) async-start(bf16[16,32,768]{2,1,0:T(8,128)(2,1)} %bitcast.16), calls=%async_computation.1 | async-start | bytes 1572864 | tf_op jit(solution)/shard_map/all_to_all | solution.py:261
  38.3 12.4 %collective-permute-start = (bf16[256,256]{1,0:T(8,128)(2,1)S(1)}, bf16[256,256]{1,0:T(8,128)(2,1)S(1)}, u32[]{:S(2)}, u32[]{:S(2)}) collective-permute-start(bf16[256,256]{1,0:T(8,128)(2,1)S(1)} %copy-done.2), channel_id=1, source_target_pairs={{0,4},{2,6},{4,8},{6,10},{8,12},{10,14},{12,16},{14,18},{16,20},{1... | collective-permute-start | bytes 393224 | tf_op jit(solution)/shard_map/ppermute | solution.py:237
  42.0 8.8 %collective-permute-start.1 = (bf16[256,256]{1,0:T(8,128)(2,1)S(1)}, bf16[256,256]{1,0:T(8,128)(2,1)S(1)}, u32[]{:S(2)}, u32[]{:S(2)}) collective-permute-start(bf16[256,256]{1,0:T(8,128)(2,1)S(1)} %copy-done.2), channel_id=1, source_target_pairs={{0,2},{2,4},{4,6},{6,8},{8,10},{10,12},{12,14},{14,16},{16,18},{18... | collective-permute-start | bytes 393224 | tf_op jit(solution)/shard_map/ppermute | solution.py:237
  43.8 14.7 %collective-permute-start.2 = (bf16[256,256]{1,0:T(8,128)(2,1)S(1)}, bf16[256,256]{1,0:T(8,128)(2,1)S(1)}, u32[]{:S(2)}, u32[]{:S(2)}) collective-permute-start(bf16[256,256]{1,0:T(8,128)(2,1)S(1)} %copy-done.3), channel_id=1, source_target_pairs={{0,4},{2,6},{4,8},{6,10},{8,12},{10,14},{12,16},{14,18},{16,20},{1... | collective-permute-start | bytes 393224 | tf_op jit(solution)/shard_map/ppermute | solution.py:237
  47.3 11.9 %collective-permute-start.3 = (bf16[256,256]{1,0:T(8,128)(2,1)S(1)}, bf16[256,256]{1,0:T(8,128)(2,1)S(1)}, u32[]{:S(2)}, u32[]{:S(2)}) collective-permute-start(bf16[256,256]{1,0:T(8,128)(2,1)S(1)} %copy-done.3), channel_id=1, source_target_pairs={{0,2},{2,4},{4,6},{6,8},{8,10},{10,12},{12,14},{14,16},{16,18},{18... | collective-permute-start | bytes 393224 | tf_op jit(solution)/shard_map/ppermute | solution.py:237
  50.6 30.2 %copy-start.11 = (s32[256]{0:T(256)S(1)}, s32[256]{0:T(256)}, u32[]{:S(2)}) copy-start(s32[256]{0:T(256)} %param.12) | copy-start | bytes 3076
  58.5 0.7 copy-start.4
  59.2 0.6 copy-start.6
  59.8 0.9 copy-start.5
  60.7 0.9 copy-start.7
  73.1 10.0 %collective-permute-start.4 = (bf16[256,2048]{1,0:T(8,128)(2,1)S(1)}, bf16[256,2048]{1,0:T(8,128)(2,1)S(1)}, u32[]{:S(2)}, u32[]{:S(2)}) collective-permute-start(bf16[256,2048]{1,0:T(8,128)(2,1)S(1)} %shard_map.95), channel_id=1, source_target_pairs={{0,2},{2,0},{4,6},{6,4},{8,10},{10,8},{12,14},{14,12},{16,18},{18,... | collective-permute-start | bytes 3145736 | tf_op jit(solution)/shard_map/ppermute | solution.py:229
  83.1 5.5 %copy-start.8 = (bf16[256,2048]{1,0:T(8,128)(2,1)}, bf16[256,2048]{1,0:T(8,128)(2,1)S(1)}, u32[]{:S(2)}) copy-start(bf16[256,2048]{1,0:T(8,128)(2,1)S(1)} %collective-permute-done.4) | copy-start | bytes 3145732
  88.6 2.4 %copy-start.9 = (f32[512,768]{0,1:T(8,128)}, f32[512,768]{0,1:T(8,128)S(1)}, u32[]{:S(2)}) copy-start(f32[512,768]{0,1:T(8,128)S(1)} %fusion.10) | copy-start | bytes 4718596
  89.5 11.3 %collective-permute-start.5 = (bf16[512,384]{0,1:T(8,128)(2,1)}, bf16[512,384]{0,1:T(8,128)(2,1)S(1)}, u32[]{:S(2)}, u32[]{:S(2)}) collective-permute-start(bf16[512,384]{0,1:T(8,128)(2,1)} %dynamic-slice_convert_fusion), channel_id=1, source_target_pairs={{0,1},{1,0},{2,3},{3,2},{4,5},{5,4},{6,7},{7,6},{8,9},{9,8},{10,11... | collective-permute-start | bytes 1179656 | tf_op jit(solution)/shard_map/ppermute | solution.py:279
  91.1 1.5 collective-permute-start.7
  102.1 1.5 collective-permute-start.6
  105.0 85.1 %all-to-all-start = ((bf16[16,32,768]{2,1,0:T(8,128)(2,1)}), bf16[16,32,768]{2,1,0:T(8,128)(2,1)S(1)}, u32[]{:S(2)}, u32[]{:S(2)}) async-start(bf16[16,32,768]{2,1,0:T(8,128)(2,1)} %bitcast.11), calls=%async_computation | async-start | bytes 1572864 | tf_op jit(solution)/shard_map/all_to_all | solution.py:289
Sparse Core Ops, SparseCore 0:
  10.2 74.6 all-gather.3
